TPU v7x, 128 devices: a whole 4x4x4 slice. The times are simulated.
128 devices in a mesh: lat: 4 (over z), lon: 32 (over x, y, core).
Axes of the slice: x: 4, y: 4, z: 4, core: 2. Of those that a mesh axis runs over, the one named last changes fastest.
Arguments:
- obs_tiles: bfloat16 [128, 128, 4, 8, 256], P(('lat', 'lon'))
- tile_block: int32 [128, 128, 4], P(('lat', 'lon')), may hold values from 0 to 11
- tile_rows: int32 [128, 128, 4], P(('lat', 'lon')), may hold values from 0 to 256, as said below
- embed_weight: bfloat16 [6, 23], replicated, may hold values from -2.5 to 2.5
- conv1_weight: bfloat16 [9, 24, 256], replicated, may hold values from -0.4375 to 0.4375
- conv1_bias: float32 [256], replicated, may hold values from -3 to 3
- conv2_weight: bfloat16 [9, 256, 512], replicated, may hold values from -0.125 to 0.125
- conv2_bias: float32 [512], replicated, may hold values from -3 to 3
Outputs:
- coarse: bfloat16 [64, 384, 512], P('lat')
Inputs may be any that keep to these rules, and one draw needn't show every extreme that they name: `tile_rows`: for each source and destination the live slots come first: all hold 256 rows but the last live one, which holds 1 to 256; later slots hold 0. In every draw one destination block receives 4 live tiles from every source.
All inputs are finite; a program needn't handle non-finite values.
Results may differ from a plain program's by a relative error of at most 0.0052.
Values may be sent and summed in bfloat16 or wider, within the bound.
No kernel may reach another device: no remote copies, remote signals or barrier semaphores. Data moves between devices by JAX's collectives and lax.ppermute only.
A program may use at most 64 MiB of HBM per device.

v0:
```python
import jax
import jax.numpy as jnp
from jax import lax
from jax.sharding import PartitionSpec as P

BX = 64
BY = 48
SB = 16
kernel_scale = 0.5


def shifted(value, axis, by):
    length = lax.axis_size(axis)
    return lax.ppermute(value, axis, [(i, (i + by) % length) for i in range(length)])


def from_behind(block, axis, distance):
    devices = range(lax.axis_size(axis))
    route = [(i - distance, i) for i in devices if i - distance in devices]
    return lax.ppermute(block, axis, route)


def tile_terms(tiles, row_count, embed_weight):
    cell_ids = jnp.arange(SB * SB, dtype=jnp.int32)
    center_row = (cell_ids // SB).astype(jnp.float32) + 0.5
    center_col = (cell_ids % SB).astype(jnp.float32) + 0.5
    place_row = tiles[:, 0, :].astype(jnp.float32)
    place_col = tiles[:, 1, :].astype(jnp.float32)
    distance = (center_row[None, :, None] - place_row[:, None, :]) ** 2 + (
        center_col[None, :, None] - place_col[:, None, :]
    ) ** 2
    is_live = jnp.arange(tiles.shape[2], dtype=jnp.int32)[None, None, :] < row_count[:, None, None]
    kernel = jnp.where(is_live, jnp.exp(-distance * kernel_scale), jnp.float32(0.0)).astype(
        jnp.bfloat16
    )
    embedded = jnp.einsum(
        "tvo,vc->tco", tiles[:, 2:, :], embed_weight, preferred_element_type=jnp.float32
    ).astype(jnp.bfloat16)
    features = jnp.concatenate(
        [jnp.ones((tiles.shape[0], 1, tiles.shape[2]), jnp.bfloat16), embedded], axis=1
    )
    return jnp.einsum("tco,tko->tck", features, kernel, preferred_element_type=jnp.float32)


def stride_conv(padded, weight, out_rows, out_cols):
    running = jnp.zeros((out_rows * out_cols, weight.shape[2]), jnp.float32)
    for row_tap in range(3):
        for col_tap in range(3):
            tap_rows = lax.slice(
                padded,
                (row_tap, col_tap, 0),
                (row_tap + 2 * out_rows - 1, col_tap + 2 * out_cols - 1, padded.shape[2]),
                (2, 2, 1),
            )
            running = running + jnp.dot(
                tap_rows.reshape(-1, padded.shape[2]),
                weight[3 * row_tap + col_tap],
                preferred_element_type=jnp.float32,
            )
    return running.reshape(out_rows, out_cols, weight.shape[2])


def shards(
    obs_tiles,
    tile_block,
    tile_rows,
    embed_weight,
    conv1_weight,
    conv1_bias,
    conv2_weight,
    conv2_bias,
):
    block_count = obs_tiles.shape[1]
    slot_count = obs_tiles.shape[2]
    feat_rows = obs_tiles.shape[3]
    tile_len = obs_tiles.shape[4]
    arrived_all = (
        lax.all_to_all(obs_tiles, ("lat", "lon"), split_axis=1, concat_axis=0, tiled=True),
        lax.all_to_all(tile_block, ("lat", "lon"), split_axis=1, concat_axis=0, tiled=True),
        lax.all_to_all(tile_rows, ("lat", "lon"), split_axis=1, concat_axis=0, tiled=True),
    )
    group_count = block_count // 8
    group_size = 8 * slot_count
    arrived = arrived_all[0].reshape(group_count, group_size, feat_rows, tile_len)
    block_ids = arrived_all[1].reshape(group_count, group_size)
    row_count = arrived_all[2].reshape(group_count, group_size)
    sub_count = BX // SB * (BY // SB)
    channel_count = conv1_weight.shape[1]

    def add_group(running, inputs):
        tiles, group_ids, group_rows = inputs
        tile_sums = tile_terms(tiles, group_rows, embed_weight)
        onehot = (group_ids[:, None] == jnp.arange(sub_count, dtype=jnp.int32)[None, :]).astype(
            jnp.float32
        )
        return (
            running + jnp.einsum("ts,tck->sck", onehot, tile_sums, precision=lax.Precision.HIGHEST),
            None,
        )

    start = jnp.zeros((sub_count, channel_count, tile_len), jnp.float32)
    block_sums, _ = lax.scan(add_group, start, (arrived, block_ids, row_count))
    density = block_sums[:, 0, :]
    data_part = block_sums[:, 1:, :] / (1.0 + density[:, None, :])
    channels = jnp.concatenate([jnp.log1p(density)[:, None, :], data_part], axis=1).astype(
        jnp.bfloat16
    )
    grid_field = (
        channels.reshape(BX // SB, BY // SB, channel_count, SB, SB)
        .transpose(0, 3, 1, 4, 2)
        .reshape(BX, BY, channel_count)
    )
    rim_width = 1
    side_rim = shifted(grid_field[:, BY - rim_width :, :], "lon", 1)
    padded = jnp.concatenate([side_rim, grid_field], axis=1)
    top_rim = from_behind(padded[BX - rim_width :, :, :], "lat", 1)
    padded = jnp.concatenate([top_rim, padded], axis=0)
    first_layer = jax.nn.silu(
        stride_conv(padded, conv1_weight, BX // 2, BY // 2) + conv1_bias
    ).astype(jnp.bfloat16)
    first_side = shifted(first_layer[:, BY // 2 - 1 :, :], "lon", 1)
    first_padded = jnp.concatenate([first_side, first_layer], axis=1)
    first_top = from_behind(first_padded[BX // 2 - 1 :, :, :], "lat", 1)
    first_padded = jnp.concatenate([first_top, first_padded], axis=0)
    coarse = (stride_conv(first_padded, conv2_weight, BX // 4, BY // 4) + conv2_bias).astype(
        jnp.bfloat16
    )
    return lax.all_gather(coarse, "lon", axis=1, tiled=True)


def solution(mesh):
    placed = (
        P(("lat", "lon"), None, None, None, None),
        P(("lat", "lon"), None, None),
        P(("lat", "lon"), None, None),
        P(),
        P(),
        P(),
        P(),
        P(),
    )
    return jax.shard_map(
        shards, mesh=mesh, in_specs=placed, out_specs=P("lat", None, None), check_vma=False
    )
```

profile of v0, /device:TPU:1, one launch (start us, length us, event | category | flops | bytes accessed | tf_op | source)
XLA Modules:
  0.0 268.7 jit_solution(6266015869091623327)
XLA Ops:
  6.5 1.4 copy.26
  8.0 11.5 %all-to-all-start = ((s32[1,128,4]{2,0,1:T(1,128)}), s32[1,128,4]{2,0,1:T(1,128)S(1)}, u32[]{:S(2)}, u32[]{:S(2)}) async-start(s32[1,128,4]{2,0,1:T(1,128)} %copy.26), calls=%async_computation | async-start | bytes 131072 | tf_op jit(solution)/shard_map/all_to_all | solution.py:79
  19.5 0.8 copy.28
  20.3 8.7 %all-to-all-done = s32[1,128,4]{2,0,1:T(1,128)S(1)} async-done(((s32[1,128,4]{2,0,1:T(1,128)}), s32[1,128,4]{2,0,1:T(1,128)S(1)}, u32[]{:S(2)}, u32[]{:S(2)}) %all-to-all-start) | async-done | bytes 2080 | tf_op jit(solution)/shard_map/all_to_all | solution.py:79
  29.0 13.8 %all_to_all.12 = s32[1,128,4]{2,0,1:T(1,128)S(1)} all-to-all(s32[1,128,4]{2,0,1:T(1,128)S(1)} %copy.28), channel_id=1, replica_groups=mesh['lat'=4,'lon'=32] {'lat','lon'}, dimensions={1} | all-to-all | bytes 4096 | tf_op jit(solution)/shard_map/all_to_all | solution.py:80
  42.8 4.4 %all-to-all-start.1 = ((bf16[1,128,4,8,256]{4,3,2,0,1:T(8,128)(2,1)}), bf16[1,128,4,8,256]{4,3,2,0,1:T(8,128)(2,1)S(1)}, u32[]{:S(2)}, u32[]{:S(2)}) async-start(bf16[1,128,4,8,256]{4,3,2,0,1:T(8,128)(2,1)} %bitcast.136), calls=%async_computation.1 | async-start | bytes 4194304 | tf_op jit(solution)/shard_map/all_to_all | solution.py:78
  47.8 0.8 reduce.6
  48.6 0.8 reduce.7
  49.5 28.2 %all-to-all-done.1 = bf16[1,128,4,8,256]{4,3,2,0,1:T(8,128)(2,1)S(1)} async-done(((bf16[1,128,4,8,256]{4,3,2,0,1:T(8,128)(2,1)}), bf16[1,128,4,8,256]{4,3,2,0,1:T(8,128)(2,1)S(1)}, u32[]{:S(2)}, u32[]{:S(2)}) %all-to-all-start.1) | async-done | bytes 2097184 | tf_op jit(solution)/shard_map/all_to_all | solution.py:78
  77.7 61.0 %while.13 = (s32[]{:T(128)}, f32[12,24,256]{2,0,1:T(8,128)S(1)}, s32[16,32]{1,0:T(8,128)S(1)}, bf16[16,32,8,256]{3,2,1,0:T(8,128)(2,1)S(1)}, bf16[6,23]{1,0:T(8,...) while((s32[]{:T(128)}, f32[12,24,256]{2,0,1:T(8,128)S(1)}, ...), condition=%wide.region_1.2_spmd.clone, body=%wide.region_0.1_spmd.clone.sunk | while | flops 150475136 | bytes 3626115 | solution.py:102
  78.2 2.7 fusion.104
  82.0 2.7 fusion.104
  85.8 2.7 fusion.104
  89.6 2.7 fusion.104
  93.5 2.7 fusion.104
  97.3 2.7 fusion.104
  101.1 2.7 fusion.104
  104.9 2.7 fusion.104
  108.7 2.7 fusion.104
  112.5 2.7 fusion.104
  116.3 2.7 fusion.104
  120.2 2.7 fusion.104
  124.0 2.7 fusion.104
  127.8 2.7 fusion.104
  131.6 2.7 fusion.104
  135.4 2.7 fusion.104
  139.0 0.8 concatenate.25
  140.0 1.1 copy.30
  141.8 1.6 slice.164
  143.4 1.7 slice.162
  145.1 0.8 slice.158
  145.9 0.8 slice.156
  146.8 0.8 collective-permute-start
  147.6 0.9 fusion.53
  148.6 1.8 fusion.51
  150.4 0.9 fusion.48
  151.3 0.9 fusion.46
  152.9 0.8 copy.31
  153.8 0.9 fusion.25
  154.7 2.0 collective-permute-start.1
  156.7 3.7 %slice.160 = bf16[32,24,24]{0,2,1:T(8,128)(2,1)S(1)} slice(bf16[64,49,24]{0,2,1:T(8,128)(2,1)S(1)} %pad_maximum_fusion.1), slice={[1:64:2], [0:47:2], [0:24:1]} | slice | bytes 73728 | tf_op jit(solution)/shard_map/slice | solution.py:49
  160.4 3.7 %slice.154 = bf16[32,24,24]{0,2,1:T(8,128)(2,1)S(1)} slice(bf16[64,49,24]{0,2,1:T(8,128)(2,1)S(1)} %pad_maximum_fusion.1), slice={[0:63:2], [0:47:2], [0:24:1]} | slice | bytes 73728 | tf_op jit(solution)/shard_map/slice | solution.py:49
  164.3 0.9 reshape.154
  165.3 0.9 reshape.157
  166.2 1.1 maximum_maximum_fusion.1
  167.3 4.2 %slice.152 = bf16[32,24,24]{0,2,1:T(8,128)(2,1)S(1)} slice(bf16[65,49,24]{0,2,1:T(8,128)(2,1)S(1)} %maximum_maximum_fusion.1), slice={[0:63:2], [2:49:2], [0:24:1]} | slice | bytes 73728 | tf_op jit(solution)/shard_map/slice | solution.py:49
  171.5 3.7 %slice.150 = bf16[32,24,24]{0,2,1:T(8,128)(2,1)S(1)} slice(bf16[65,49,24]{0,2,1:T(8,128)(2,1)S(1)} %maximum_maximum_fusion.1), slice={[0:63:2], [1:48:2], [0:24:1]} | slice | bytes 73728 | tf_op jit(solution)/shard_map/slice | solution.py:49
  175.2 3.7 %slice.148 = bf16[32,24,24]{0,2,1:T(8,128)(2,1)S(1)} slice(bf16[65,49,24]{0,2,1:T(8,128)(2,1)S(1)} %maximum_maximum_fusion.1), slice={[0:63:2], [0:47:2], [0:24:1]} | slice | bytes 73728 | tf_op jit(solution)/shard_map/slice | solution.py:49
  179.4 0.9 reshape.151
  180.8 1.1 fusion.58
  181.8 1.0 convolution_add_fusion.4
  182.8 1.0 convolution_add_fusion.3
  183.9 1.0 fusion.23
  184.9 1.0 fusion.24
  186.3 0.7 slice.184
  187.0 0.8 slice.182
  188.6 0.7 reshape.169
  189.3 0.7 reshape.168
  191.9 2.1 collective-permute-start.3
  194.2 0.7 slice.180
  196.0 1.0 maximum_maximum_fusion
  200.5 0.8 copy.38
  201.4 51.4 %all-gather.2.cloned.1.call-done = bf16[16,384,512]{2,0,1:T(8,128)(2,1)} async-done(((bf16[16,12,512]{2,0,1:T(8,128)(2,1)}), bf16[16,384,512]{2,0,1:T(8,128)(2,1)}) %all-gather.2.cloned.1.call-update) | async-done | bytes 6291472 | tf_op jit(solution)/shard_map/all_gather | solution.py:128
  252.8 9.0 %copy.39 = bf16[16,384,512]{2,1,0:T(8,128)(2,1)} copy(bf16[16,384,512]{2,0,1:T(8,128)(2,1)} %all-gather.2.cloned.1.call-done) | data formatting | bytes 12582912 | tf_op jit(solution)/shard_map/all_gather | solution.py:128
  (208 shorter events, 29.1 us)
Async XLA Ops:
  8.0 21.0 %all-to-all-start = ((s32[1,128,4]{2,0,1:T(1,128)}), s32[1,128,4]{2,0,1:T(1,128)S(1)}, u32[]{:S(2)}, u32[]{:S(2)}) async-start(s32[1,128,4]{2,0,1:T(1,128)} %copy.26), calls=%async_computation | async-start | bytes 131072 | tf_op jit(solution)/shard_map/all_to_all | solution.py:79
  20.2 57.5 %copy-start.10 = (bf16[6,23]{1,0:T(8,128)(2,1)S(1)}, bf16[6,23]{1,0:T(8,128)(2,1)}, u32[]{:S(2)}) copy-start(bf16[6,23]{1,0:T(8,128)(2,1)} %param.13) | copy-start | bytes 832
  42.8 34.9 %all-to-all-start.1 = ((bf16[1,128,4,8,256]{4,3,2,0,1:T(8,128)(2,1)}), bf16[1,128,4,8,256]{4,3,2,0,1:T(8,128)(2,1)S(1)}, u32[]{:S(2)}, u32[]{:S(2)}) async-start(bf16[1,128,4,8,256]{4,3,2,0,1:T(8,128)(2,1)} %bitcast.136), calls=%async_computation.1 | async-start | bytes 4194304 | tf_op jit(solution)/shard_map/all_to_all | solution.py:78
  47.2 205.6 %all-gather.2.cloned.1.call-start = ((), (), s32[]{:S(2)}) async-start(), calls=%async_computation.3 | async-start | bytes 6488064 | tf_op jit(solution)/shard_map/all_gather | solution.py:128
  146.8 6.2 %collective-permute-start = (bf16[64,1,24]{2,1,0:T(2,128)(2,1)}, bf16[64,1,24]{2,1,0:T(2,128)(2,1)}, u32[]{:S(2)}, u32[]{:S(2)}) collective-permute-start(bf16[64,1,24]{2,1,0:T(2,128)(2,1)} %slice.192), channel_id=1, source_target_pairs={{0,1},{1,2},{2,3},{3,4},{4,5},{5,6},{6,7},{7,8},{8,9},{9,10},{10,1... | collective-permute-start | bytes 9224 | tf_op jit(solution)/shard_map/ppermute | solution.py:14
  154.7 11.5 %collective-permute-start.1 = (bf16[1,49,24]{0,2,1:T(8,128)(2,1)}, bf16[1,49,24]{0,2,1:T(8,128)(2,1)}, u32[]{:S(2)}, u32[]{:S(2)}) collective-permute-start(bf16[1,49,24]{0,2,1:T(8,128)(2,1)} %fusion.25), channel_id=1, source_target_pairs={{0,32},{32,64},{64,96},{1,33},{33,65},{65,97},{2,34},{34,66},{66,9... | collective-permute-start | bytes 7064 | tf_op jit(solution)/shard_map/ppermute | solution.py:20
  180.3 3.5 %copy-start = (f32[768,256]{1,0:T(8,128)S(1)}, f32[768,256]{1,0:T(8,128)}, u32[]{:S(2)}) copy-start(f32[768,256]{1,0:T(8,128)} %fusion.51) | copy-start | bytes 2359300
  180.5 3.4 %copy-start.9 = (bf16[768,24]{0,1:T(8,128)(2,1)S(1)}, bf16[768,24]{0,1:T(8,128)(2,1)}, u32[]{:S(2)}) copy-start(bf16[768,24]{0,1:T(8,128)(2,1)} %reshape.154) | copy-start | bytes 110596
  182.8 2.1 copy-start.8
  184.9 1.0 copy-start.12
  186.2 5.1 %collective-permute-start.2 = (bf16[32,1,256]{2,1,0:T(2,128)(2,1)S(1)}, bf16[32,1,256]{2,1,0:T(2,128)(2,1)S(1)}, u32[]{:S(2)}, u32[]{:S(2)}) collective-permute-start(bf16[32,1,256]{2,1,0:T(2,128)(2,1)S(1)} %slice.195), channel_id=1, source_target_pairs={{0,1},{1,2},{2,3},{3,4},{4,5},{5,6},{6,7},{7,8},{8,9},{9,10},{10,1... | collective-permute-start | bytes 49160 | tf_op jit(solution)/shard_map/ppermute | solution.py:14
  191.3 7.1 %copy-start.1 = (bf16[9,256,512]{2,1,0:T(8,128)(2,1)S(1)}, bf16[9,256,512]{2,1,0:T(8,128)(2,1)}, u32[]{:S(2)}) copy-start(bf16[9,256,512]{2,1,0:T(8,128)(2,1)} %param.16) | copy-start | bytes 7077892
  191.3 2.7 copy-start.7
  191.9 4.1 %collective-permute-start.3 = (bf16[1,25,256]{2,1,0:T(8,128)(2,1)}, bf16[1,25,256]{2,1,0:T(8,128)(2,1)S(1)}, u32[]{:S(2)}, u32[]{:S(2)}) collective-permute-start(bf16[1,25,256]{2,1,0:T(8,128)(2,1)} %fusion.45), channel_id=1, source_target_pairs={{0,32},{32,64},{64,96},{1,33},{33,65},{65,97},{2,34},{34,66},{66,9... | collective-permute-start | bytes 38408 | tf_op jit(solution)/shard_map/ppermute | solution.py:20
  197.0 2.0 copy-start.6
  198.3 1.0 copy-start.5
  198.6 0.9 copy-start.4
  199.1 0.9 copy-start.3
  199.3 0.9 copy-start.2
  199.7 0.7 copy-start.11
Sparse Core Ops, SparseCore 0:
  201.5 51.2 all-gather.1
where the time goes:
time: 270 us; the launch traced here: 269 us
  waiting for transfers between devices  88.4 us (33%)
  matrix products  69.2 us (26%)
  local copies, waits for them, and re-layouts  53.3 us (20%)
  starting transfers between devices  20.9 us (8%)
  between operations  14 us (5%)
  blocking collectives  13.8 us (5%)
  other arithmetic  7.95 us (3%)
    all_gather x1, waiting for transfers between devices, shards(): return lax.all_gather(coarse, 'lon', axis=1, tiled=True)  51.4 us
    dot_general x16, matrix products, tile_terms(): jnp.einsum('tco,tko->tck', features, kernel, preferred_element_type=jnp.f...  42.6 us
    slice x23, local copies, waits for them, and re-layouts, stride_conv(): lax.slice(padded, (row_tap, col_tap, 0), (row_tap + 2 * out_rows - 1, col...  29.3 us
    all_to_all x1, waiting for transfers between devices, shards(): lax.all_to_all(obs_tiles, ('lat', 'lon'), split_axis=1, concat_axis=0, ti...  28.2 us
    all_to_all x1, blocking collectives, shards(): lax.all_to_all(tile_rows, ('lat', 'lon'), split_axis=1, concat_axis=0, ti...  13.8 us
    dot_general x18, matrix products, stride_conv(): jnp.dot(tap_rows.reshape(-1, padded.shape[2]), weight[3 * row_tap + col_t...  11.6 us
    all_to_all x1, starting transfers between devices, shards(): lax.all_to_all(tile_block, ('lat', 'lon'), split_axis=1, concat_axis=0, t...  11.5 us
    dot_general x16, matrix products, add_group(): jnp.einsum('ts,tck->sck', onehot, tile_sums, precision=lax.Precision.HIGH...  10.1 us
  transfers between devices with their start and end apart: 7, of which 3 were waited for; matrix products, arithmetic and copies ran while one was open for 9% of the time, Pallas kernels for 0%

commit v1 on v0

--- a/solution.py
+++ b/solution.py
@@ -2,6 +2,7 @@
 import jax.numpy as jnp
 from jax import lax
 from jax.sharding import PartitionSpec as P
+from jax.lax import all_to_all, axis_size
 
 BX = 64
 BY = 48
@@ -125,7 +126,9 @@
     coarse = (stride_conv(first_padded, conv2_weight, BX // 4, BY // 4) + conv2_bias).astype(
         jnp.bfloat16
     )
-    return lax.all_gather(coarse, "lon", axis=1, tiled=True)
+    return jnp.concatenate(
+        all_to_all(jnp.stack([coarse for _ in range(axis_size("lon"))]), "lon", 0, 0), 1
+    )
 
 
 def solution(mesh):

time: 270 us -> 283 us (1.048)
  blocking collectives: 13.8 us -> 95.3 us
  waiting for transfers between devices: 88.4 us -> 37 us
  between operations: 14 us -> 0.67 us
  local copies, waits for them, and re-layouts: 53.3 us -> 49.4 us
    all_to_all x0 -> x1, blocking collectives: none -> 81.5 us  [shards(): all_to_all(jnp.stack([coarse for _ in range(axis_size('lon'))]), 'lon', 0...]
    all_gather x1 -> x0, waiting for transfers between devices: 51.4 us -> none  [shards(): return lax.all_gather(coarse, 'lon', axis=1, tiled=True)]
    all_gather x1 -> x0, local copies, waits for them, and re-layouts: 9.02 us -> none  [shards(): return lax.all_gather(coarse, 'lon', axis=1, tiled=True)]
    reshape x0 -> x1, local copies, waits for them, and re-layouts: none -> 6.36 us  [shards(): jnp.concatenate(all_to_all(jnp.stack([coarse for _ in range(axis_size('lo...]
  transfers between devices with their start and end apart: 7 -> 6, of which waited for: 3 -> 2; matrix products, arithmetic and copies ran while one was open for 9% -> 9% of each run, Pallas kernels for 0% -> 0%
where the time goes in v1:
time: 283 us; the launch traced here: 281 us
  blocking collectives  95.3 us (34%)
  matrix products  69.2 us (24%)
  local copies, waits for them, and re-layouts  49.4 us (17%)
  waiting for transfers between devices  37 us (13%)
  starting transfers between devices  20.9 us (7%)
  other arithmetic  7.96 us (3%)
    all_to_all x1, blocking collectives, shards(): all_to_all(jnp.stack([coarse for _ in range(axis_size('lon'))]), 'lon', 0...  81.5 us
    dot_general x16, matrix products, tile_terms(): jnp.einsum('tco,tko->tck', features, kernel, preferred_element_type=jnp.f...  42.6 us
    slice x23, local copies, waits for them, and re-layouts, stride_conv(): lax.slice(padded, (row_tap, col_tap, 0), (row_tap + 2 * out_rows - 1, col...  29.4 us
    all_to_all x1, waiting for transfers between devices, shards(): lax.all_to_all(obs_tiles, ('lat', 'lon'), split_axis=1, concat_axis=0, ti...  28.2 us
    all_to_all x1, blocking collectives, shards(): lax.all_to_all(tile_rows, ('lat', 'lon'), split_axis=1, concat_axis=0, ti...  13.8 us
    dot_general x18, matrix products, stride_conv(): jnp.dot(tap_rows.reshape(-1, padded.shape[2]), weight[3 * row_tap + col_t...  11.6 us
    all_to_all x1, starting transfers between devices, shards(): lax.all_to_all(tile_block, ('lat', 'lon'), split_axis=1, concat_axis=0, t...  11.5 us
    dot_general x16, matrix products, add_group(): jnp.einsum('ts,tck->sck', onehot, tile_sums, precision=lax.Precision.HIGH...  10.1 us
  transfers between devices with their start and end apart: 6, of which 2 were waited for; matrix products, arithmetic and copies ran while one was open for 9% of the time, Pallas kernels for 0%

profile of v1, /device:TPU:1, one launch (start us, length us, event | category | flops | bytes accessed | tf_op | source)
XLA Modules:
  0.0 281.4 jit_solution(16323616203619833429)
XLA Ops:
  0.0 1.4 copy.28
  1.4 11.5 %all-to-all-start = ((s32[1,128,4]{2,0,1:T(1,128)}), s32[1,128,4]{2,0,1:T(1,128)S(1)}, u32[]{:S(2)}, u32[]{:S(2)}) async-start(s32[1,128,4]{2,0,1:T(1,128)} %copy.28), calls=%async_computation | async-start | bytes 131072 | tf_op jit(solution)/shard_map/all_to_all | solution.py:80
  12.9 0.8 copy.30
  13.7 8.7 %all-to-all-done = s32[1,128,4]{2,0,1:T(1,128)S(1)} async-done(((s32[1,128,4]{2,0,1:T(1,128)}), s32[1,128,4]{2,0,1:T(1,128)S(1)}, u32[]{:S(2)}, u32[]{:S(2)}) %all-to-all-start) | async-done | bytes 2080 | tf_op jit(solution)/shard_map/all_to_all | solution.py:80
  22.5 13.8 %all_to_all.32 = s32[1,128,4]{2,0,1:T(1,128)S(1)} all-to-all(s32[1,128,4]{2,0,1:T(1,128)S(1)} %copy.30), channel_id=1, replica_groups=mesh['lat'=4,'lon'=32] {'lat','lon'}, dimensions={1} | all-to-all | bytes 4096 | tf_op jit(solution)/shard_map/all_to_all | solution.py:81
  36.3 4.4 %all-to-all-start.1 = ((bf16[1,128,4,8,256]{4,3,2,0,1:T(8,128)(2,1)}), bf16[1,128,4,8,256]{4,3,2,0,1:T(8,128)(2,1)S(1)}, u32[]{:S(2)}, u32[]{:S(2)}) async-start(bf16[1,128,4,8,256]{4,3,2,0,1:T(8,128)(2,1)} %bitcast.140), calls=%async_computation.1 | async-start | bytes 4194304 | tf_op jit(solution)/shard_map/all_to_all | solution.py:79
  41.2 0.8 reduce.6
  42.1 0.8 reduce.7
  42.9 28.2 %all-to-all-done.1 = bf16[1,128,4,8,256]{4,3,2,0,1:T(8,128)(2,1)S(1)} async-done(((bf16[1,128,4,8,256]{4,3,2,0,1:T(8,128)(2,1)}), bf16[1,128,4,8,256]{4,3,2,0,1:T(8,128)(2,1)S(1)}, u32[]{:S(2)}, u32[]{:S(2)}) %all-to-all-start.1) | async-done | bytes 2097184 | tf_op jit(solution)/shard_map/all_to_all | solution.py:79
  71.2 61.0 %while.13 = (s32[]{:T(128)}, f32[12,24,256]{2,0,1:T(8,128)S(1)}, s32[16,32]{1,0:T(8,128)S(1)}, bf16[16,32,8,256]{3,2,1,0:T(8,128)(2,1)S(1)}, bf16[6,23]{1,0:T(8,...) while((s32[]{:T(128)}, f32[12,24,256]{2,0,1:T(8,128)S(1)}, ...), condition=%wide.region_1.2_spmd.clone, body=%wide.region_0.1_spmd.clone.sunk | while | flops 150475136 | bytes 3626115 | solution.py:103
  71.7 2.7 fusion.104
  75.5 2.7 fusion.104
  79.3 2.7 fusion.104
  83.1 2.7 fusion.104
  86.9 2.7 fusion.104
  90.7 2.7 fusion.104
  94.6 2.7 fusion.104
  98.4 2.7 fusion.104
  102.2 2.7 fusion.104
  106.0 2.7 fusion.104
  109.8 2.7 fusion.104
  113.6 2.7 fusion.104
  117.4 2.7 fusion.104
  121.3 2.7 fusion.104
  125.1 2.7 fusion.104
  128.9 2.7 fusion.104
  132.4 0.8 concatenate.25
  133.5 1.1 copy.32
  134.6 1.7 slice.164
  136.3 1.7 slice.162
  138.0 0.8 slice.158
  138.8 0.8 slice.156
  139.7 0.8 collective-permute-start
  140.5 0.9 fusion.53
  141.5 1.8 fusion.51
  143.3 0.9 fusion.48
  144.2 0.9 fusion.46
  145.9 0.9 fusion.25
  146.8 2.0 collective-permute-start.1
  148.9 3.7 %slice.160 = bf16[32,24,24]{0,2,1:T(8,128)(2,1)S(1)} slice(bf16[64,49,24]{0,2,1:T(8,128)(2,1)S(1)} %pad_maximum_fusion.1), slice={[1:64:2], [0:47:2], [0:24:1]} | slice | bytes 73728 | tf_op jit(solution)/shard_map/slice | solution.py:50
  152.6 3.7 %slice.154 = bf16[32,24,24]{0,2,1:T(8,128)(2,1)S(1)} slice(bf16[64,49,24]{0,2,1:T(8,128)(2,1)S(1)} %pad_maximum_fusion.1), slice={[0:63:2], [0:47:2], [0:24:1]} | slice | bytes 73728 | tf_op jit(solution)/shard_map/slice | solution.py:50
  156.4 0.9 reshape.163
  157.5 0.9 reshape.166
  158.3 1.1 maximum_maximum_fusion.1
  159.5 4.2 %slice.152 = bf16[32,24,24]{0,2,1:T(8,128)(2,1)S(1)} slice(bf16[65,49,24]{0,2,1:T(8,128)(2,1)S(1)} %maximum_maximum_fusion.1), slice={[0:63:2], [2:49:2], [0:24:1]} | slice | bytes 73728 | tf_op jit(solution)/shard_map/slice | solution.py:50
  163.7 3.7 %slice.150 = bf16[32,24,24]{0,2,1:T(8,128)(2,1)S(1)} slice(bf16[65,49,24]{0,2,1:T(8,128)(2,1)S(1)} %maximum_maximum_fusion.1), slice={[0:63:2], [1:48:2], [0:24:1]} | slice | bytes 73728 | tf_op jit(solution)/shard_map/slice | solution.py:50
  167.3 3.7 %slice.148 = bf16[32,24,24]{0,2,1:T(8,128)(2,1)S(1)} slice(bf16[65,49,24]{0,2,1:T(8,128)(2,1)S(1)} %maximum_maximum_fusion.1), slice={[0:63:2], [0:47:2], [0:24:1]} | slice | bytes 73728 | tf_op jit(solution)/shard_map/slice | solution.py:50
  171.6 0.9 reshape.160
  172.9 1.1 fusion.58
  174.0 1.0 convolution_add_fusion.4
  175.0 1.0 convolution_add_fusion.3
  176.0 1.0 fusion.23
  177.0 1.0 fusion.24
  178.4 0.7 slice.184
  179.1 0.8 slice.182
  180.8 0.7 reshape.178
  182.7 0.7 reshape.174
  184.0 2.1 collective-permute-start.3
  186.3 0.7 slice.180
  187.4 0.7 reshape.173
  188.1 1.0 maximum_maximum_fusion
  192.8 0.8 stack.2
  193.6 81.5 %all_to_all.33 = bf16[32,16,12,512]{3,1,2,0:T(8,128)(2,1)S(1)} all-to-all(bf16[32,16,12,512]{3,1,2,0:T(8,128)(2,1)S(1)} %stack.2), channel_id=1, replica_groups=mesh['lat'=4,'lon'=32] {'lon'}, dimensions={0} | all-to-all | bytes 12582912 | tf_op jit(solution)/shard_map/all_to_all | solution.py:130
  275.1 6.4 %copy.41 = bf16[16,384,512]{2,1,0:T(8,128)(2,1)} copy(bf16[16,384,512]{2,0,1:T(8,128)(2,1)S(1)} %bitcast.131) | data formatting | bytes 12582912 | tf_op jit(solution)/shard_map/reshape | solution.py:129
  (207 shorter events, 27.9 us)
Async XLA Ops:
  1.4 21.0 %all-to-all-start = ((s32[1,128,4]{2,0,1:T(1,128)}), s32[1,128,4]{2,0,1:T(1,128)S(1)}, u32[]{:S(2)}, u32[]{:S(2)}) async-start(s32[1,128,4]{2,0,1:T(1,128)} %copy.28), calls=%async_computation | async-start | bytes 131072 | tf_op jit(solution)/shard_map/all_to_all | solution.py:80
  13.7 57.5 %copy-start.10 = (bf16[6,23]{1,0:T(8,128)(2,1)S(1)}, bf16[6,23]{1,0:T(8,128)(2,1)}, u32[]{:S(2)}) copy-start(bf16[6,23]{1,0:T(8,128)(2,1)} %param.13) | copy-start | bytes 832
  36.3 34.9 %all-to-all-start.1 = ((bf16[1,128,4,8,256]{4,3,2,0,1:T(8,128)(2,1)}), bf16[1,128,4,8,256]{4,3,2,0,1:T(8,128)(2,1)S(1)}, u32[]{:S(2)}, u32[]{:S(2)}) async-start(bf16[1,128,4,8,256]{4,3,2,0,1:T(8,128)(2,1)} %bitcast.140), calls=%async_computation.1 | async-start | bytes 4194304 | tf_op jit(solution)/shard_map/all_to_all | solution.py:79
  139.7 6.2 %collective-permute-start = (bf16[64,1,24]{2,1,0:T(2,128)(2,1)S(1)}, bf16[64,1,24]{2,1,0:T(2,128)(2,1)S(1)}, u32[]{:S(2)}, u32[]{:S(2)}) collective-permute-start(bf16[64,1,24]{2,1,0:T(2,128)(2,1)S(1)} %slice.192), channel_id=1, source_target_pairs={{0,1},{1,2},{2,3},{3,4},{4,5},{5,6},{6,7},{7,8},{8,9},{9,10},{10,1... | collective-permute-start | bytes 9224 | tf_op jit(solution)/shard_map/ppermute | solution.py:15
  146.8 11.5 %collective-permute-start.1 = (bf16[1,49,24]{0,2,1:T(8,128)(2,1)}, bf16[1,49,24]{0,2,1:T(8,128)(2,1)}, u32[]{:S(2)}, u32[]{:S(2)}) collective-permute-start(bf16[1,49,24]{0,2,1:T(8,128)(2,1)} %fusion.25), channel_id=1, source_target_pairs={{0,32},{32,64},{64,96},{1,33},{33,65},{65,97},{2,34},{34,66},{66,9... | collective-permute-start | bytes 7064 | tf_op jit(solution)/shard_map/ppermute | solution.py:21
  172.5 3.5 %copy-start = (f32[768,256]{1,0:T(8,128)S(1)}, f32[768,256]{1,0:T(8,128)}, u32[]{:S(2)}) copy-start(f32[768,256]{1,0:T(8,128)} %fusion.51) | copy-start | bytes 2359300
  172.6 3.4 %copy-start.9 = (bf16[768,24]{0,1:T(8,128)(2,1)S(1)}, bf16[768,24]{0,1:T(8,128)(2,1)}, u32[]{:S(2)}) copy-start(bf16[768,24]{0,1:T(8,128)(2,1)} %reshape.163) | copy-start | bytes 110596
  175.0 2.1 copy-start.8
  177.0 1.0 copy-start.12
  178.3 5.1 %collective-permute-start.2 = (bf16[32,1,256]{2,1,0:T(2,128)(2,1)S(1)}, bf16[32,1,256]{2,1,0:T(2,128)(2,1)S(1)}, u32[]{:S(2)}, u32[]{:S(2)}) collective-permute-start(bf16[32,1,256]{2,1,0:T(2,128)(2,1)S(1)} %slice.195), channel_id=1, source_target_pairs={{0,1},{1,2},{2,3},{3,4},{4,5},{5,6},{6,7},{7,8},{8,9},{9,10},{10,1... | collective-permute-start | bytes 49160 | tf_op jit(solution)/shard_map/ppermute | solution.py:15
  183.4 7.1 %copy-start.1 = (bf16[9,256,512]{2,1,0:T(8,128)(2,1)S(1)}, bf16[9,256,512]{2,1,0:T(8,128)(2,1)}, u32[]{:S(2)}) copy-start(bf16[9,256,512]{2,1,0:T(8,128)(2,1)} %param.16) | copy-start | bytes 7077892
  183.4 2.7 copy-start.7
  184.0 4.1 %collective-permute-start.3 = (bf16[1,25,256]{2,1,0:T(8,128)(2,1)}, bf16[1,25,256]{2,1,0:T(8,128)(2,1)S(1)}, u32[]{:S(2)}, u32[]{:S(2)}) collective-permute-start(bf16[1,25,256]{2,1,0:T(8,128)(2,1)} %fusion.45), channel_id=1, source_target_pairs={{0,32},{32,64},{64,96},{1,33},{33,65},{65,97},{2,34},{34,66},{66,9... | collective-permute-start | bytes 38408 | tf_op jit(solution)/shard_map/ppermute | solution.py:21
  189.1 2.0 copy-start.6
  190.4 1.0 copy-start.5
  190.7 0.9 copy-start.4
  191.2 0.9 copy-start.3
  191.4 0.9 copy-start.2
  191.8 0.7 copy-start.11
